TPU v7x, 32 devices: a whole 2x2x4 slice. The times are simulated.
32 devices in a mesh: chan: 2 (over x), src: 16 (over z, y, core).
Axes of the slice: x: 2, y: 2, z: 4, core: 2. Of those that a mesh axis runs over, the one named last changes fastest.
Arguments:
- intensity: float32 [65536], P(('chan', 'src')), parts along dimension 0, may hold values from 0.25 to 4
- directions: float32 [4, 3, 32768], P(None, None, 'src'), may hold values from -1 to 1
- positions: float32 [6, 350], P('chan'), parts along dimension 0, may hold values from -20 to 20
- beam: bfloat16 [350, 512], P(None, 'src'), may hold values from 0.19921875 to 1
- need: int32 [4, 128], P(None, 'src'), may hold values from 0 to 31
- knot_index: int32 [4, 4, 32768], P(None, None, 'src'), may hold values from 0 to 127
- knot_weight: float32 [4, 4, 32768], P(None, None, 'src'), may hold values from 0 to 1
- pairs: int32 [2, 7680], P(None, 'src'), may hold values from 0 to 349, as said below
Outputs:
- vis: float32 [8, 2, 7680], P('chan', None, 'src'), parts along dimension 0
There are 2 independent parts, one for each index of `chan`. A program takes and returns all parts, laid end to end along the dimension named above; an argument that names none is the same for every part. Nothing has to cross between parts.
Inputs may be any that keep to these rules, and one draw needn't show every extreme that they name: `pairs`: each listed pair names two antennas, the first below the second.
All inputs are finite; a program needn't handle non-finite values.
Results may differ from a plain program's by a relative error of at most 0.004.
Values may be sent and summed in bfloat16 or wider, within the bound.
A program may use at most 256 MiB of HBM per device.

v0:
```python
import jax
import jax.numpy as jnp
from jax import lax
from jax.experimental import pallas as pl
from jax.experimental.pallas import tpu as pltpu
from jax.sharding import PartitionSpec as P

TIME_STEPS = 4
PATCH_PIXELS = 16
NEED = 8
KNOTS = 4
SLOTS = NEED * PATCH_PIXELS
CHUNK = 512
BF = jnp.bfloat16
F32 = jnp.float32
MAGIC = 12582912.0

SIN = (4.4428679, -7.30744342, 3.59478805, -0.78437398)
COS = (-1.41420408, 6.97764205, -5.71523832, 1.72834847)


def nt(a, b):
    return lax.dot_general(a, b, (((1,), (1,)), ((), ())), preferred_element_type=F32)


def pieces(x):
    hi = x.astype(BF).astype(F32)
    mid = (x - hi).astype(BF).astype(F32)
    return hi, mid, (x - hi) - mid


def gram_kernel(scale, ants, rows, wide, need_ref, intensity_ref, directions_ref, positions_ref, beam_ref,
                index_ref, weight_ref, out_ref, pos, beam_sel, amp, s0, s1, gram):
    count = intensity_ref.shape[1]
    chunks = count // CHUNK
    amp[...] = jnp.sqrt(intensity_ref[...]) * scale
    s0[...] = jnp.zeros_like(s0)
    s1[...] = jnp.zeros_like(s1)
    gram[...] = jnp.zeros_like(gram)
    p0, p1, p2 = pieces(positions_ref[...])
    pos[...] = jnp.concatenate([p0, p0, p1, p1, p0, p2], axis=0).T.astype(BF)
    slots = (s0, s1)
    iota = lax.broadcasted_iota(jnp.int32, (SLOTS, CHUNK), 0)

    def fill(t, c, slot):
        lanes = pl.ds(c * CHUNK, CHUNK)
        d0, d1, d2 = pieces(directions_ref[t, :, lanes])
        d = jnp.concatenate([d0, d1, d0, d1, d2, d0], axis=0).astype(BF)
        u = jnp.dot(pos[:rows], d, preferred_element_type=F32)
        spread = jnp.zeros((SLOTS, CHUNK), F32)
        a = amp[:, lanes]
        for k in range(KNOTS):
            w = weight_ref[t, pl.ds(k, 1), lanes] * a
            spread = spread + jnp.where(iota == index_ref[t, pl.ds(k, 1), lanes], w, 0.0)
        hi = spread.astype(BF)
        lo = (spread - hi.astype(F32)).astype(BF)
        b = beam_sel[:rows]
        amount = jnp.dot(
            jnp.concatenate([b, b], axis=1), jnp.concatenate([hi, lo], axis=0), preferred_element_type=F32
        )
        r = u - ((u + MAGIC) - MAGIC)
        z = r * r
        s = (((SIN[3] * z + SIN[2]) * z + SIN[1]) * z + SIN[0]) * r
        n = ((COS[3] * z + COS[2]) * z + COS[1]) * z + COS[0]
        q = amount * s
        slot[:rows] = (amount - q * s).astype(BF)
        slot[wide : wide + rows] = (q * n).astype(BF)

    def add(slot):
        for lo in range(0, 2 * wide, 256):
            hi = min(lo + 256, 2 * wide)
            cols = slot[lo:hi]
            if lo < rows:
                gram[lo:rows, lo:hi] += nt(slot[lo:rows], cols)
            top = max(lo, wide)
            gram[top : wide + rows, lo:hi] += nt(slot[top : wide + rows], cols)

    def finish(t):
        w = gram[wide:, :wide]
        real = gram[:wide, :wide] + gram[wide:, wide:]
        r = lax.broadcasted_iota(jnp.int32, (wide, wide), 0)
        c = lax.broadcasted_iota(jnp.int32, (wide, wide), 1)
        out_ref[t] = jnp.where(r > c, real, w - w.T)
        gram[...] = jnp.zeros_like(gram)

    def body(t, carry):
        picked = [
            beam_ref[pl.ds(pl.multiple_of(need_ref[t, j] * PATCH_PIXELS, PATCH_PIXELS), PATCH_PIXELS), :]
            for j in range(NEED)
        ]
        beam_sel[...] = jnp.concatenate(picked, axis=0).astype(F32).T.astype(BF)
        for c in range(chunks):
            fill(t, c, slots[c % 2])
            add(slots[(c + 1) % 2])
            if c == 0:
                @pl.when(t > 0)
                def _():
                    finish(t - 1)
        return carry

    lax.fori_loop(0, TIME_STEPS, body, 0)
    add(slots[(chunks - 1) % 2])
    finish(TIME_STEPS - 1)


def pick_kernel(pairs_ref, total_ref, out_ref):
    wide = total_ref.shape[1]
    count = pairs_ref.shape[1]
    iota = lax.broadcasted_iota(jnp.int32, (wide, count), 0)
    first = iota == pairs_ref[0:1, :]
    second = iota == pairs_ref[1:2, :]
    one0 = jnp.where(first, 1.0, 0.0).astype(BF)
    one1 = jnp.where(second, 1.0, 0.0).astype(BF)
    for t in range(TIME_STEPS):
        v = total_ref[t]
        hi = v.astype(BF)
        lo = (v - hi.astype(F32)).astype(BF)
        both = jnp.concatenate([hi, lo], axis=1)
        for part, (one, mask) in enumerate(((one0, second), (one1, first))):
            x = jnp.dot(both, jnp.concatenate([one, one], axis=0), preferred_element_type=F32)
            out_ref[t, part : part + 1, :] = jnp.sum(jnp.where(mask, x, 0.0), axis=0, keepdims=True)


def local(intensity, directions, positions, beam, need, knot_index, knot_weight, pairs):
    ants = positions.shape[1]
    rows = -(-ants // 16) * 16
    wide = -(-ants // 128) * 128
    count = intensity.shape[0]
    scale = float(count * lax.axis_size("src")) ** (-0.25)
    mine = jnp.pad(beam.T, ((0, 0), (0, wide - ants)))
    whole = lax.all_gather(mine, "src", axis=0, tiled=True)
    spaced = jnp.pad(positions, ((0, 5), (0, wide - ants)))
    aimed = jnp.pad(directions, ((0, 0), (0, 5), (0, 0)))
    vmem = pl.BlockSpec(memory_space=pltpu.VMEM)
    part = pl.pallas_call(
        lambda *refs: gram_kernel(scale, ants, rows, wide, *refs),
        out_shape=jax.ShapeDtypeStruct((TIME_STEPS, wide, wide), F32),
        in_specs=[pl.BlockSpec(memory_space=pltpu.SMEM)] + [vmem] * 6,
        out_specs=vmem,
        scratch_shapes=[
            pltpu.VMEM((wide, 48), BF),
            pltpu.VMEM((wide, SLOTS), BF),
            pltpu.VMEM((1, count), F32),
            pltpu.VMEM((2 * wide, CHUNK), BF),
            pltpu.VMEM((2 * wide, CHUNK), BF),
            pltpu.VMEM((2 * wide, 2 * wide), F32),
        ],
        compiler_params=pltpu.CompilerParams(vmem_limit_bytes=56 * 1024 * 1024),
    )(need, intensity.reshape(1, count), aimed, spaced, whole, knot_index, knot_weight)
    total = lax.psum(part, "src")
    return pl.pallas_call(
        pick_kernel,
        out_shape=jax.ShapeDtypeStruct((TIME_STEPS, 2, pairs.shape[1]), F32),
        in_specs=[vmem, vmem],
        out_specs=vmem,
        compiler_params=pltpu.CompilerParams(vmem_limit_bytes=56 * 1024 * 1024),
    )(pairs, total)


def solution(mesh):
    placed = (
        P(("chan", "src")),
        P(None, None, "src"),
        P("chan", None),
        P(None, "src"),
        P(None, "src"),
        P(None, None, "src"),
        P(None, None, "src"),
        P(None, "src"),
    )
    return jax.shard_map(
        local, mesh=mesh, in_specs=placed, out_specs=P("chan", None, "src"), check_vma=False
    )
```

profile of v0, /device:TPU:0, one launch (start us, length us, event | category | flops | bytes accessed | tf_op | source)
XLA Modules:
  0.0 164.3 jit_solution(18411196468011469463)
XLA Ops:
  6.5 0.0 all-reduce.5.cloned.1.call-start
  6.5 1.0 copy.9
  7.5 1.3 pad.13.refs_3_
  8.8 0.7 pad.12.refs_2_
  9.5 0.7 pad.14
  10.3 25.7 %all_gather.3.refs_4_ = bf16[512,384]{1,0:T(8,128)(2,1)} all-gather(bf16[32,384]{1,0:T(8,128)(2,1)S(1)} %pad.14), channel_id=1, replica_groups=mesh['chan'=2,'src'=16] {'src'}, dimensions={0}, use_global_device_ids=true | all-gather | bytes 417792 | tf_op jit(solution)/shard_map/all_gather | solution.py:131
  36.0 19.8 %shard_map.82 = f32[4,384,384]{2,1,0:T(8,128)} custom-call(s32[4,8]{1,0:T(4,128)} %refs_0_.1, f32[1,2048]{1,0:T(1,128)} %bitcast.3, f32[4,8,2048]{2,1,0:T(8,128)} %pad.12.refs_2_, f32[8,384]{1,0:T(8,128)} %pad.13.refs_3_, bf16[512,384]{1,0:T(8,128)(2,1)} %all_gather.3.refs_4_, s32[4,4,2048]{2,1,0:T(4,128)} %refs_5_.1, f32[4,4,2048]{2,1,0:T(4,128)} %refs_6_.1), custom_call_target="tpu_custom_call" | custom-call | tf_op jit(solution)/shard_map/pallas_call | solution.py:135
  55.8 0.0 all-reduce.5.cloned.1.call-update
  55.8 96.6 %all-reduce.5.cloned.1.call-done.total_ref = f32[4,384,384]{2,1,0:T(8,128)} async-done(((f32[4,384,384]{2,1,0:T(8,128)}), f32[4,384,384]{2,1,0:T(8,128)}) %all-reduce.5.cloned.1.call-update) | async-done | bytes 2359312 | tf_op jit(solution)/shard_map/psum | solution.py:150
  152.4 5.1 %shard_map.83 = f32[4,2,480]{2,1,0:T(2,128)} custom-call(s32[2,480]{1,0:T(2,128)} %pairs_ref.1, f32[4,384,384]{2,1,0:T(8,128)} %all-reduce.5.cloned.1.call-done.total_ref), custom_call_target="tpu_custom_call" | custom-call | tf_op jit(solution)/shard_map/pallas_call | solution.py:151
Async XLA Ops:
  6.5 145.9 %all-reduce.5.cloned.1.call-start = ((), (), s32[]{:S(2)}) async-start(), calls=%async_computation | async-start | bytes 4718592 | tf_op jit(solution)/shard_map/psum | solution.py:150
Sparse Core Ops, SparseCore 0:
  55.9 96.4 all-reduce.4
where the time goes:
time: 165 us; the launch traced here: 164 us
  waiting for transfers between devices  96.6 us (59%)
  blocking collectives  25.7 us (16%)
  Pallas kernels  24.8 us (15%)
  between operations  13.4 us (8%)
  local copies, waits for them, and re-layouts  3.73 us (2%)
    psum x1, waiting for transfers between devices, local(): total = lax.psum(part, 'src')  96.6 us
    all_gather x1, blocking collectives, local(): whole = lax.all_gather(mine, 'src', axis=0, tiled=True)  25.7 us
    pallas_call x1, Pallas kernels, local(): pl.pallas_call(lambda *refs: gram_kernel(scale, ants, rows, wide, *refs),...  19.8 us
    pallas_call x1, Pallas kernels, local(): pl.pallas_call(pick_kernel, out_shape=jax.ShapeDtypeStruct((TIME_STEPS, 2...  5.08 us
  transfers between devices with their start and end apart: 1, of which 1 were waited for; matrix products, arithmetic and copies ran while one was open for 0% of the time, Pallas kernels for 0%

commit v1 on v0

--- a/solution.py
+++ b/solution.py
@@ -103,22 +103,115 @@
     finish(TIME_STEPS - 1)
 
 
-def pick_kernel(pairs_ref, total_ref, out_ref):
-    wide = total_ref.shape[1]
-    count = pairs_ref.shape[1]
+def partners(size):
+    me = lax.axis_index("src")
+    flips = [1 << bit for bit in range(size.bit_length() - 1)]
+    return me, flips
+
+
+def flip(me, value):
+    return me + value - 2 * value * (lax.div(me, value) % 2)
+
+
+def greet(others):
+    barrier = pltpu.get_barrier_semaphore()
+    for other in others:
+        pl.semaphore_signal(barrier, inc=1, device_id={"src": other}, device_id_type=pl.DeviceIdType.MESH)
+    pl.semaphore_wait(barrier, len(others))
+
+
+def push(src, dst, send, recv, other):
+    copy = pltpu.make_async_remote_copy(
+        src_ref=src, dst_ref=dst, send_sem=send, recv_sem=recv,
+        device_id={"src": other}, device_id_type=pl.DeviceIdType.MESH,
+    )
+    copy.start()
+    return copy
+
+
+def reverse(index, bits):
+    out = 0
+    for bit in range(bits):
+        out = out + (index // (1 << bit)) % 2 * (1 << (bits - 1 - bit))
+    return out
+
+
+def spread_kernel(size, beam_ref, pairs_ref, whole_ref, quad_ref, sems, quad_sems):
+    me, flips = partners(size)
+    bits = len(flips)
+    quad = [flip(me, 1), flip(me, 2), flip(flip(me, 1), 2)]
+    slot = reverse(me, bits)
+    whole_ref[slot] = beam_ref[...]
+    quad_ref[me % 4] = pairs_ref[...]
+    greet([flip(me, value) for value in flips[2:]] + quad)
+    copies = []
+    for j, other in enumerate(quad):
+        copies.append(push(pairs_ref, quad_ref.at[me % 4], quad_sems.at[0, j], quad_sems.at[1, j], other))
+    for stage in range(bits):
+        held = 1 << stage
+        blocks = whole_ref.at[pl.ds(slot // held * held, held)]
+        push(blocks, blocks, sems.at[0, stage], sems.at[1, stage], flip(me, flips[bits - 1 - stage])).wait()
+    for copy in copies:
+        copy.wait()
+
+
+def total_kernel(size, part_ref, quad_ref, out_ref, ones, got0, send1, got1, acc, sends, gots, res, got, sem0, sem1, sems,
+                 quad_sems):
+    me, flips = partners(size)
+    wide = part_ref.shape[1]
+    half, quarter = wide // 2, wide // 4
+    count = quad_ref.shape[2]
+    core, side = me % 2, me // 2 % 2
+    quad = [flip(me, 1), flip(me, 2), flip(flip(me, 1), 2)]
+    greet([flip(me, value) for value in flips[2:]] + quad)
+    first = []
+    for t in range(TIME_STEPS):
+        away = part_ref.at[t, pl.ds(pl.multiple_of((1 - core) * half, 64), half)]
+        first.append(push(away, got0.at[t], sem0.at[0, t], sem0.at[1, t], quad[0]))
     iota = lax.broadcasted_iota(jnp.int32, (wide, count), 0)
-    first = iota == pairs_ref[0:1, :]
-    second = iota == pairs_ref[1:2, :]
-    one0 = jnp.where(first, 1.0, 0.0).astype(BF)
-    one1 = jnp.where(second, 1.0, 0.0).astype(BF)
+    for m in range(4):
+        for k in range(2):
+            ones[m, k] = jnp.where(iota == quad_ref[m, k : k + 1, :], 1.0, 0.0).astype(BF)
+    mine = pl.multiple_of(core * half + side * quarter, 32)
+    theirs = pl.multiple_of(core * half + (1 - side) * quarter, 32)
+    in_mine = pl.multiple_of(side * quarter, 32)
+    in_theirs = pl.multiple_of((1 - side) * quarter, 32)
+    second = []
     for t in range(TIME_STEPS):
-        v = total_ref[t]
-        hi = v.astype(BF)
-        lo = (v - hi.astype(F32)).astype(BF)
-        both = jnp.concatenate([hi, lo], axis=1)
-        for part, (one, mask) in enumerate(((one0, second), (one1, first))):
-            x = jnp.dot(both, jnp.concatenate([one, one], axis=0), preferred_element_type=F32)
-            out_ref[t, part : part + 1, :] = jnp.sum(jnp.where(mask, x, 0.0), axis=0, keepdims=True)
+        first[t].wait()
+        send1[t] = (part_ref[t, pl.ds(theirs, quarter)] + got0[t, pl.ds(in_theirs, quarter)]).astype(BF)
+        second.append(push(send1.at[t], got1.at[t], sem1.at[0, t], sem1.at[1, t], quad[1]))
+    for t in range(TIME_STEPS):
+        acc[t] = part_ref[t, pl.ds(mine, quarter)] + got0[t, pl.ds(in_mine, quarter)]
+    waiting = second
+    for stage, value in enumerate(flips[2:]):
+        later = []
+        for t in range(TIME_STEPS):
+            waiting[t].wait()
+            arrived = got1[t] if stage == 0 else gots[stage - 1, t]
+            v = acc[t] + arrived.astype(F32)
+            acc[t] = v
+            sends[stage, t] = v.astype(BF)
+            later.append(push(sends.at[stage, t], gots.at[stage, t], sems.at[0, stage, t], sems.at[1, stage, t], flip(me, value)))
+        waiting = later
+    for t in range(TIME_STEPS):
+        waiting[t].wait()
+    rows = (acc[...] + gots[len(flips) - 3].astype(F32)).astype(BF).reshape(TIME_STEPS * quarter, wide)
+    local_iota = lax.broadcasted_iota(jnp.int32, (quarter, count), 0) + mine
+    member = me % 4
+    for m in range(4):
+        for k in range(2):
+            x = jnp.dot(rows, ones[m, 1 - k], preferred_element_type=F32)
+            mask = local_iota == quad_ref[m, k : k + 1, :]
+            for t in range(TIME_STEPS):
+                y = jnp.where(mask, x[t * quarter : (t + 1) * quarter], 0.0)
+                res[m, 2 * t + 1 - k : 2 * t + 2 - k, :] = jnp.sum(y, axis=0, keepdims=True)
+    last = []
+    for j, other in enumerate(quad):
+        last.append(push(res.at[other % 4], got.at[j], quad_sems.at[0, j], quad_sems.at[1, j], other))
+    for copy in last:
+        copy.wait()
+    out_ref[...] = res[member] + got[0] + got[1] + got[2]
 
 
 def local(intensity, directions, positions, beam, need, knot_index, knot_weight, pairs):
@@ -128,10 +221,25 @@
     count = intensity.shape[0]
     scale = float(count * lax.axis_size("src")) ** (-0.25)
     mine = jnp.pad(beam.T, ((0, 0), (0, wide - ants)))
-    whole = lax.all_gather(mine, "src", axis=0, tiled=True)
+    size = lax.axis_size("src")
+    bits = size.bit_length() - 1
+    vmem = pl.BlockSpec(memory_space=pltpu.VMEM)
+    whole, quad = pl.pallas_call(
+        lambda *refs: spread_kernel(size, *refs),
+        out_shape=(
+            jax.ShapeDtypeStruct((size,) + mine.shape, BF),
+            jax.ShapeDtypeStruct((4,) + pairs.shape, jnp.int32),
+        ),
+        in_specs=[vmem, vmem],
+        out_specs=(vmem, vmem),
+        scratch_shapes=[pltpu.SemaphoreType.DMA((2, bits)), pltpu.SemaphoreType.DMA((2, 3))],
+        compiler_params=pltpu.CompilerParams(collective_id=0, has_side_effects=True),
+    )(mine, pairs)
+    parts = mine.shape[0] // PATCH_PIXELS
+    need = reverse(need // parts, bits) * parts + need % parts
+    whole = whole.reshape(-1, wide)
     spaced = jnp.pad(positions, ((0, 5), (0, wide - ants)))
     aimed = jnp.pad(directions, ((0, 0), (0, 5), (0, 0)))
-    vmem = pl.BlockSpec(memory_space=pltpu.VMEM)
     part = pl.pallas_call(
         lambda *refs: gram_kernel(scale, ants, rows, wide, *refs),
         out_shape=jax.ShapeDtypeStruct((TIME_STEPS, wide, wide), F32),
@@ -147,14 +255,33 @@
         ],
         compiler_params=pltpu.CompilerParams(vmem_limit_bytes=56 * 1024 * 1024),
     )(need, intensity.reshape(1, count), aimed, spaced, whole, knot_index, knot_weight)
-    total = lax.psum(part, "src")
-    return pl.pallas_call(
-        pick_kernel,
-        out_shape=jax.ShapeDtypeStruct((TIME_STEPS, 2, pairs.shape[1]), F32),
+    half, quarter, pair_count = wide // 2, wide // 4, pairs.shape[1]
+    dma = pltpu.SemaphoreType.DMA
+    out = pl.pallas_call(
+        lambda *refs: total_kernel(size, *refs),
+        out_shape=jax.ShapeDtypeStruct((2 * TIME_STEPS, pair_count), F32),
         in_specs=[vmem, vmem],
         out_specs=vmem,
-        compiler_params=pltpu.CompilerParams(vmem_limit_bytes=56 * 1024 * 1024),
-    )(pairs, total)
+        scratch_shapes=[
+            pltpu.VMEM((4, 2, wide, pair_count), BF),
+            pltpu.VMEM((TIME_STEPS, half, wide), F32),
+            pltpu.VMEM((TIME_STEPS, quarter, wide), BF),
+            pltpu.VMEM((TIME_STEPS, quarter, wide), BF),
+            pltpu.VMEM((TIME_STEPS, quarter, wide), F32),
+            pltpu.VMEM((bits - 2, TIME_STEPS, quarter, wide), BF),
+            pltpu.VMEM((bits - 2, TIME_STEPS, quarter, wide), BF),
+            pltpu.VMEM((4, 2 * TIME_STEPS, pair_count), F32),
+            pltpu.VMEM((3, 2 * TIME_STEPS, pair_count), F32),
+            dma((2, TIME_STEPS)),
+            dma((2, TIME_STEPS)),
+            dma((2, bits - 2, TIME_STEPS)),
+            dma((2, 3)),
+        ],
+        compiler_params=pltpu.CompilerParams(
+            collective_id=1, has_side_effects=True, vmem_limit_bytes=48 * 1024 * 1024
+        ),
+    )(part, quad)
+    return out.reshape(TIME_STEPS, 2, pair_count)
 
 
 def solution(mesh):

time: 165 us -> 76 us (0.46)
  waiting for transfers between devices: 96.6 us -> 0 us
  Pallas kernels: 24.8 us -> 67.7 us
  blocking collectives: 25.7 us -> 0 us
  between operations: 13.4 us -> 0.03 us
  local copies, waits for them, and re-layouts: 3.73 us -> 6.62 us
    psum x1 -> x0, waiting for transfers between devices: 96.6 us -> none  [local(): total = lax.psum(part, 'src')]
    pallas_call x1 -> x2, Pallas kernels: 5.08 us -> 48 us  [the longest x1 31.1 us: local(): pl.pallas_call(lambda *refs: total_kernel(size, *refs), out_shape=jax.Sha...]
    all_gather x1 -> x0, blocking collectives: 25.7 us -> none  [local(): whole = lax.all_gather(mine, 'src', axis=0, tiled=True)]
    unnamed x1 -> x5, local copies, waits for them, and re-layouts: 0.96 us -> 2.63 us
  transfers between devices with their start and end apart: 1 -> 0, of which waited for: 1 -> 0; matrix products, arithmetic and copies ran while one was open for 0% -> 0% of each run, Pallas kernels for 0% -> 0%
where the time goes in v1:
time: 76 us; the launch traced here: 75.7 us
  Pallas kernels  67.7 us (89%)
  local copies, waits for them, and re-layouts  6.62 us (9%)
  other arithmetic  1.28 us (2%)
    pallas_call x1, Pallas kernels, local(): pl.pallas_call(lambda *refs: total_kernel(size, *refs), out_shape=jax.Sha...  31.1 us
    pallas_call x1, Pallas kernels, local(): pl.pallas_call(lambda *refs: gram_kernel(scale, ants, rows, wide, *refs),...  19.8 us
    pallas_call x1, Pallas kernels, local(): pl.pallas_call(lambda *refs: spread_kernel(size, *refs), out_shape=(jax.S...  16.8 us
    unnamed x5, local copies, waits for them, and re-layouts  2.63 us

profile of v1, /device:TPU:0, one launch (start us, length us, event | category | flops | bytes accessed | tf_op | source)
XLA Modules:
  0.0 75.7 jit_solution(5579957274424386797)
XLA Ops:
  0.0 1.3 %fusion.5.refs_0_ = s32[4,8]{1,0:T(4,128)} fusion(s32[4,8]{1,0:T(4,128)} %param.12), kind=kLoop, calls=%fused_computation.30 | loop fusion | flops 3168 | bytes 256 | tf_op jit(solution)/shard_map/add | solution.py:239
  1.3 1.3 %pad.13.refs_3_ = f32[8,384]{1,0:T(8,128)} pad(f32[3,350]{1,0:T(4,128)} %param.10, f32[]{:T(128)} %constant.90.clone.1), padding=0_5x0_34 | pad | bytes 16492 | tf_op jit(solution)/shard_map/jit(_pad)/pad | solution.py:241
  2.6 1.4 %pad.14.refs_0_ = bf16[32,384]{1,0:T(8,128)(2,1)} pad(bf16[32,350]{1,0:T(8,128)(2,1)} %bitcast.4, bf16[]{:T(256)} %constant.91.clone.1), padding=0_0x0_34 | pad | bytes 46978 | tf_op jit(solution)/shard_map/jit(_pad)/pad | solution.py:223
  3.9 1.0 %copy.9 = f32[4,3,2048]{2,1,0:T(4,128)S(1)} copy(f32[4,3,2048]{2,0,1:T(4,128)} %param.9) | data formatting | bytes 196608 | tf_op args[1]
  4.9 0.7 pad.12.refs_2_
  5.6 16.8 %shard_map.82 = (bf16[16,32,384]{2,1,0:T(8,128)(2,1)}, s32[4,2,480]{2,1,0:T(2,128)}) custom-call(bf16[32,384]{1,0:T(8,128)(2,1)} %pad.14.refs_0_, s32[2,480]{1,0:T(2,128)} %refs_1_.1), custom_call_target="tpu_custom_call" | custom-call | tf_op jit(solution)/shard_map/pallas_call | solution.py:227
  22.4 0.0 copy-start.1
  22.5 19.8 %shard_map.83.refs_0_ = f32[4,384,384]{2,1,0:T(8,128)} custom-call(s32[4,8]{1,0:T(4,128)} %fusion.5.refs_0_, f32[1,2048]{1,0:T(1,128)} %bitcast.5, f32[4,8,2048]{2,1,0:T(8,128)} %pad.12.refs_2_, f32[8,384]{1,0:T(8,128)} %pad.13.refs_3_, bf16[512,384]{1,0:T(8,128)(2,1)} %bitcast.3, s32[4,4,2048]{2,1,0:T(4,128)} %refs_5_.1, f32[4,4,2048]{2,1,0:T(4,128)} %refs_6_.1), custom_call_target="tpu_custom_call" | custom-call | tf_op jit(solution)/shard_map/pallas_call | solution.py:243
  42.2 0.0 copy-done.1
  42.2 0.0 copy-start
  42.2 1.7 %copy-done = f32[4,384,384]{2,1,0:T(8,128)S(1)} copy-done((f32[4,384,384]{2,1,0:T(8,128)S(1)}, f32[4,384,384]{2,1,0:T(8,128)}, u32[]{:S(2)}) %copy-start) | copy-done | bytes 2359320
  43.9 31.1 %shard_map.84 = f32[8,480]{1,0:T(8,128)S(1)} custom-call(f32[4,384,384]{2,1,0:T(8,128)S(1)} %copy-done, s32[4,2,480]{2,1,0:T(2,128)S(1)} %copy-done.1), custom_call_target="tpu_custom_call" | custom-call | tf_op jit(solution)/shard_map/pallas_call | solution.py:260
  75.0 0.6 reshape.11
Async XLA Ops:
  22.4 19.8 %copy-start.1 = (s32[4,2,480]{2,1,0:T(2,128)S(1)}, s32[4,2,480]{2,1,0:T(2,128)}, u32[]{:S(2)}) copy-start(s32[4,2,480]{2,1,0:T(2,128)} %get-tuple-element.8.refs_1_) | copy-start | bytes 46084
  42.2 1.7 %copy-start = (f32[4,384,384]{2,1,0:T(8,128)S(1)}, f32[4,384,384]{2,1,0:T(8,128)}, u32[]{:S(2)}) copy-start(f32[4,384,384]{2,1,0:T(8,128)} %shard_map.83.refs_0_) | copy-start | bytes 7077892

commit v2 on v0

v2 whole, which is shorter than its diff:
```python
import jax
import jax.numpy as jnp
from jax import lax
from jax.experimental import pallas as pl
from jax.experimental.pallas import tpu as pltpu
from jax.sharding import PartitionSpec as P

TIME_STEPS = 4
PATCH_PIXELS = 16
NEED = 8
KNOTS = 4
SLOTS = NEED * PATCH_PIXELS
CHUNK = 512
BF = jnp.bfloat16
F32 = jnp.float32
MAGIC = 12582912.0

SIN = (4.4428679, -7.30744342, 3.59478805, -0.78437398)
COS = (-1.41420408, 6.97764205, -5.71523832, 1.72834847)


def nt(a, b):
    return lax.dot_general(a, b, (((1,), (1,)), ((), ())), preferred_element_type=F32)


def pieces(x):
    hi = x.astype(BF).astype(F32)
    mid = (x - hi).astype(BF).astype(F32)
    return hi, mid, (x - hi) - mid


def partners(size):
    me = lax.axis_index("src")
    flips = [1 << bit for bit in range(size.bit_length() - 1)]
    return me, flips


def flip(me, value):
    return me + value - 2 * value * (lax.div(me, value) % 2)


def greet(others):
    barrier = pltpu.get_barrier_semaphore()
    for other in others:
        pl.semaphore_signal(barrier, inc=1, device_id={"src": other}, device_id_type=pl.DeviceIdType.MESH)
    pl.semaphore_wait(barrier, len(others))


def push(src, dst, send, recv, other):
    copy = pltpu.make_async_remote_copy(
        src_ref=src, dst_ref=dst, send_sem=send, recv_sem=recv,
        device_id={"src": other}, device_id_type=pl.DeviceIdType.MESH,
    )
    copy.start()
    return copy


def reverse(index, bits):
    out = 0
    for bit in range(bits):
        out = out + (index // (1 << bit)) % 2 * (1 << (bits - 1 - bit))
    return out


def kernel(size, scale, need_ref, intensity_ref, directions_ref, positions_ref, beam_ref, index_ref, weight_ref,
           pairs_ref, out_ref, whole, quads, pos, padded, block, dirs, beam_sel, amp, s0, s1, gram, kept_s, kept_n, part,
           ones, got0, send1, got1, acc, sends, gots, res, got, gsem, qsem, sem0, sem1, sems, rsem):
    me, flips = partners(size)
    bits = len(flips)
    count = intensity_ref.shape[1]
    chunks = count // CHUNK
    ants = positions_ref.shape[1]
    depth = beam_ref.shape[1]
    parts = depth // PATCH_PIXELS
    rows, wide = -(-ants // 16) * 16, whole.shape[2]
    half, quarter = wide // 2, wide // 4
    pair_count = pairs_ref.shape[1]
    core, side = me % 2, me // 2 % 2
    quad = [flip(me, 1), flip(me, 2), flip(flip(me, 1), 2)]

    slot_me = reverse(me, bits)
    block[...] = jnp.zeros_like(block)
    block[:ants, :depth] = beam_ref[...].astype(F32)
    whole[slot_me] = block[...].T[:depth].astype(BF)
    quads[me % 4] = pairs_ref[...]
    greet([flip(me, value) for value in flips[2:]] + quad)

    def gather_copy(stage):
        held = 1 << stage
        blocks = whole.at[pl.ds(slot_me // held * held, held)]
        return pltpu.make_async_remote_copy(
            src_ref=blocks, dst_ref=blocks, send_sem=gsem.at[0, stage], recv_sem=gsem.at[1, stage],
            device_id={"src": flip(me, flips[bits - 1 - stage])}, device_id_type=pl.DeviceIdType.MESH,
        )

    gather_copy(0).start()
    listed = [
        push(pairs_ref, quads.at[me % 4], qsem.at[0, j], qsem.at[1, j], other) for j, other in enumerate(quad)
    ]

    amp[...] = jnp.sqrt(intensity_ref[...]) * scale
    s0[...] = jnp.zeros_like(s0)
    s1[...] = jnp.zeros_like(s1)
    gram[...] = jnp.zeros_like(gram)
    dirs[...] = jnp.zeros_like(dirs)
    padded[...] = jnp.zeros_like(padded)
    padded[0:3, :ants] = positions_ref[...]
    p0, p1, p2 = pieces(padded[...])
    pos[...] = jnp.concatenate([p0, p0, p1, p1, p0, p2], axis=0).T.astype(BF)
    slots = (s0, s1)
    iota = lax.broadcasted_iota(jnp.int32, (SLOTS, CHUNK), 0)

    def fringe(t, c):
        lanes = pl.ds(c * CHUNK, CHUNK)
        d0, d1, d2 = pieces(directions_ref[t, :, lanes])
        for j, d in enumerate((d0, d1, d0, d1, d2, d0)):
            dirs[c % 2, 8 * j : 8 * j + 3] = d
        u = jnp.dot(pos[:rows], dirs[c % 2].astype(BF), preferred_element_type=F32)
        r = u - ((u + MAGIC) - MAGIC)
        z = r * r
        s = (((SIN[3] * z + SIN[2]) * z + SIN[1]) * z + SIN[0]) * r
        n = ((COS[3] * z + COS[2]) * z + COS[1]) * z + COS[0]
        return s, n

    def fill(t, c, slot, kept):
        lanes = pl.ds(c * CHUNK, CHUNK)
        spread = jnp.zeros((SLOTS, CHUNK), F32)
        a = amp[:, lanes]
        for k in range(KNOTS):
            w = weight_ref[t, pl.ds(k, 1), lanes] * a
            spread = spread + jnp.where(iota == index_ref[t, pl.ds(k, 1), lanes], w, 0.0)
        hi = spread.astype(BF)
        lo = (spread - hi.astype(F32)).astype(BF)
        b = beam_sel[:rows]
        amount = jnp.dot(
            jnp.concatenate([b, b], axis=1), jnp.concatenate([hi, lo], axis=0), preferred_element_type=F32
        )
        if kept:
            s, n = kept_s[:, lanes], kept_n[:, lanes]
        else:
            s, n = fringe(t, c)
        q = amount * s
        slot[:rows] = (amount - q * s).astype(BF)
        slot[wide : wide + rows] = (q * n).astype(BF)

    def add(slot):
        for lo in range(0, 2 * wide, 256):
            hi = min(lo + 256, 2 * wide)
            cols = slot[lo:hi]
            if lo < rows:
                gram[lo:rows, lo:hi] += nt(slot[lo:rows], cols)
            top = max(lo, wide)
            gram[top : wide + rows, lo:hi] += nt(slot[top : wide + rows], cols)

    def finish(t):
        w = gram[wide:, :wide]
        real = gram[:wide, :wide] + gram[wide:, wide:]
        r = lax.broadcasted_iota(jnp.int32, (wide, wide), 0)
        c = lax.broadcasted_iota(jnp.int32, (wide, wide), 1)
        part[t] = jnp.where(r > c, real, w - w.T)
        gram[...] = jnp.zeros_like(gram)

    mine = pl.multiple_of(core * half + side * quarter, 32)
    theirs = pl.multiple_of(core * half + (1 - side) * quarter, 32)
    in_mine = pl.multiple_of(side * quarter, 32)
    in_theirs = pl.multiple_of((1 - side) * quarter, 32)

    def remote(src, dst, send, recv, other):
        return pltpu.make_async_remote_copy(
            src_ref=src, dst_ref=dst, send_sem=send, recv_sem=recv,
            device_id={"src": other}, device_id_type=pl.DeviceIdType.MESH,
        )

    def core_copy(t):
        away = part.at[t, pl.ds(pl.multiple_of((1 - core) * half, 64), half)]
        return remote(away, got0.at[t], sem0.at[0, t], sem0.at[1, t], quad[0])

    def side_copy(t):
        return remote(send1.at[t], got1.at[t], sem1.at[0, t], sem1.at[1, t], quad[1])

    def far_copy(t, e):
        return remote(
            sends.at[e, t], gots.at[e, t], sems.at[0, e, t], sems.at[1, e, t], flip(me, flips[2 + e])
        )

    def to_side(t):
        core_copy(t).wait()
        send1[t] = (part[t, pl.ds(theirs, quarter)] + got0[t, pl.ds(in_theirs, quarter)]).astype(BF)
        side_copy(t).start()
        acc[t] = part[t, pl.ds(mine, quarter)] + got0[t, pl.ds(in_mine, quarter)]

    def to_far(t, e):
        if e == 0:
            side_copy(t).wait()
            v = acc[t] + got1[t].astype(F32)
        else:
            far_copy(t, e - 1).wait()
            v = acc[t] + gots[e - 1, t].astype(F32)
        acc[t] = v
        sends[e, t] = v.astype(BF)
        far_copy(t, e).start()

    for stage in range(max(bits, chunks)):
        if stage < chunks:
            lanes = pl.ds(stage * CHUNK, CHUNK)
            kept_s[:, lanes], kept_n[:, lanes] = fringe(0, stage)
        if stage < bits:
            gather_copy(stage).wait()
            if stage + 1 < bits:
                gather_copy(stage + 1).start()
    for copy in listed:
        copy.wait()

    pair_iota = lax.broadcasted_iota(jnp.int32, (wide, pair_count), 0)

    pixel = lax.broadcasted_iota(jnp.int32, (PATCH_PIXELS, size * depth), 1)
    row = lax.broadcasted_iota(jnp.int32, (PATCH_PIXELS, size * depth), 0)

    def choose(t):
        picked = []
        for j in range(NEED):
            patch = need_ref[t, j]
            at = reverse(patch // parts, bits) * depth + patch % parts * PATCH_PIXELS
            picked.append(jnp.where(pixel - row == at, 1.0, 0.0))
        hot = jnp.concatenate(picked, axis=0).astype(BF)
        got_rows = jnp.dot(hot, whole[...].reshape(size * depth, wide), preferred_element_type=F32)
        beam_sel[...] = got_rows.T.astype(BF)
        for k in range(2):
            ones[t, k] = jnp.where(pair_iota == quads[t, k : k + 1, :], 1.0, 0.0).astype(BF)

    choose(0)
    for c in range(chunks):
        fill(0, c, slots[c % 2], True)
        if c > 0:
            add(slots[(c + 1) % 2])

    def body(t, carry):
        choose(t)
        for c in range(chunks):
            fill(t, c, slots[c % 2], False)
            add(slots[(c + 1) % 2])
            if c == 0:
                finish(t - 1)
                core_copy(t - 1).start()

                @pl.when(t > 1)
                def _():
                    to_far(t - 2, 0)
            if c == 2:
                to_side(t - 1)

                @pl.when(t > 1)
                def _():
                    to_far(t - 2, 1)
        return carry

    lax.fori_loop(1, TIME_STEPS, body, 0)
    add(slots[(chunks - 1) % 2])
    finish(TIME_STEPS - 1)
    core_copy(TIME_STEPS - 1).start()
    far = bits - 2
    to_far(TIME_STEPS - 2, 0)
    to_side(TIME_STEPS - 1)
    to_far(TIME_STEPS - 2, 1)
    to_far(TIME_STEPS - 1, 0)
    to_far(TIME_STEPS - 1, 1)
    for e in range(2, far):
        for t in range(TIME_STEPS):
            to_far(t, e)
    for t in range(TIME_STEPS):
        far_copy(t, far - 1).wait()
    total = (acc[...] + gots[far - 1].astype(F32)).astype(BF).reshape(TIME_STEPS * quarter, wide)
    local_iota = lax.broadcasted_iota(jnp.int32, (quarter, pair_count), 0) + mine
    for m in range(4):
        for k in range(2):
            x = jnp.dot(total, ones[m, 1 - k], preferred_element_type=F32)
            mask = local_iota == quads[m, k : k + 1, :]
            for t in range(TIME_STEPS):
                y = jnp.where(mask, x[t * quarter : (t + 1) * quarter], 0.0)
                res[m, 2 * t + 1 - k : 2 * t + 2 - k, :] = jnp.sum(y, axis=0, keepdims=True)
    last = []
    for j, other in enumerate(quad):
        last.append(push(res.at[other % 4], got.at[j], rsem.at[0, j], rsem.at[1, j], other))
    for copy in last:
        copy.wait()
    values = res[me % 4] + got[0] + got[1] + got[2]
    for i in range(2 * TIME_STEPS):
        out_ref[i // 2, i % 2 : i % 2 + 1, :] = values[i : i + 1]


def local(intensity, directions, positions, beam, need, knot_index, knot_weight, pairs):
    ants = positions.shape[1]
    rows = -(-ants // 16) * 16
    wide = -(-ants // 128) * 128
    count = intensity.shape[0]
    size = lax.axis_size("src")
    scale = float(count * size) ** (-0.25)
    bits = size.bit_length() - 1
    half, quarter, pair_count = wide // 2, wide // 4, pairs.shape[1]
    vmem = pl.BlockSpec(memory_space=pltpu.VMEM)
    dma = pltpu.SemaphoreType.DMA
    return pl.pallas_call(
        lambda *refs: kernel(size, scale, *refs),
        out_shape=jax.ShapeDtypeStruct((TIME_STEPS, 2, pair_count), F32),
        in_specs=[pl.BlockSpec(memory_space=pltpu.SMEM)] + [vmem] * 7,
        out_specs=vmem,
        scratch_shapes=[
            pltpu.VMEM((size, beam.shape[1], wide), BF),
            pltpu.VMEM((4, 2, pair_count), jnp.int32),
            pltpu.VMEM((wide, 48), BF),
            pltpu.VMEM((8, wide), F32),
            pltpu.VMEM((wide, 128), F32),
            pltpu.VMEM((2, 48, CHUNK), F32),
            pltpu.VMEM((wide, SLOTS), BF),
            pltpu.VMEM((1, count), F32),
            pltpu.VMEM((2 * wide, CHUNK), BF),
            pltpu.VMEM((2 * wide, CHUNK), BF),
            pltpu.VMEM((2 * wide, 2 * wide), F32),
            pltpu.VMEM((rows, count), F32),
            pltpu.VMEM((rows, count), F32),
            pltpu.VMEM((TIME_STEPS, wide, wide), F32),
            pltpu.VMEM((4, 2, wide, pair_count), BF),
            pltpu.VMEM((TIME_STEPS, half, wide), F32),
            pltpu.VMEM((TIME_STEPS, quarter, wide), BF),
            pltpu.VMEM((TIME_STEPS, quarter, wide), BF),
            pltpu.VMEM((TIME_STEPS, quarter, wide), F32),
            pltpu.VMEM((bits - 2, TIME_STEPS, quarter, wide), BF),
            pltpu.VMEM((bits - 2, TIME_STEPS, quarter, wide), BF),
            pltpu.VMEM((4, 2 * TIME_STEPS, pair_count), F32),
            pltpu.VMEM((3, 2 * TIME_STEPS, pair_count), F32),
            dma((2, bits)),
            dma((2, 3)),
            dma((2, TIME_STEPS)),
            dma((2, TIME_STEPS)),
            dma((2, bits - 2, TIME_STEPS)),
            dma((2, 3)),
        ],
        compiler_params=pltpu.CompilerParams(
            collective_id=0, has_side_effects=True, vmem_limit_bytes=56 * 1024 * 1024
        ),
    )(need, intensity.reshape(1, count), directions, positions, beam, knot_index, knot_weight, pairs)


def solution(mesh):
    placed = (
        P(("chan", "src")),
        P(None, None, "src"),
        P("chan", None),
        P(None, "src"),
        P(None, "src"),
        P(None, None, "src"),
        P(None, None, "src"),
        P(None, "src"),
    )
    return jax.shard_map(
        local, mesh=mesh, in_specs=placed, out_specs=P("chan", None, "src"), check_vma=False
    )
```

time: 165 us -> 63 us (0.38)
  waiting for transfers between devices: 96.6 us -> 0 us
  Pallas kernels: 24.8 us -> 59.2 us
  blocking collectives: 25.7 us -> 0 us
  between operations: 13.4 us -> 0.01 us
    psum x1 -> x0, waiting for transfers between devices: 96.6 us -> none  [local(): total = lax.psum(part, 'src')]
    pallas_call x2 -> x1, Pallas kernels: 24.8 us -> 59.2 us  [local(): pl.pallas_call(lambda *refs: kernel(size, scale, *refs), out_shape=jax.Sh...]
    all_gather x1 -> x0, blocking collectives: 25.7 us -> none  [local(): whole = lax.all_gather(mine, 'src', axis=0, tiled=True)]
    pad x3 -> x0, local copies, waits for them, and re-layouts: 2.76 us -> none  [the longest x1 1.3 us: local(): spaced = jnp.pad(positions, ((0, 5), (0, wide - ants)))]
    unnamed x1 -> x5, local copies, waits for them, and re-layouts: 0.96 us -> 3.55 us
  transfers between devices with their start and end apart: 1 -> 0, of which waited for: 1 -> 0; matrix products, arithmetic and copies ran while one was open for 0% -> 0% of each run, Pallas kernels for 0% -> 0%
where the time goes in v2:
time: 63 us; the launch traced here: 62.8 us
  Pallas kernels  59.2 us (94%)
  local copies, waits for them, and re-layouts  3.55 us (6%)
    pallas_call x1, Pallas kernels, local(): pl.pallas_call(lambda *refs: kernel(size, scale, *refs), out_shape=jax.Sh...  59.2 us
    unnamed x5, local copies, waits for them, and re-layouts  3.55 us

profile of v2, /device:TPU:0, one launch (start us, length us, event | category | flops | bytes accessed | tf_op | source)
XLA Modules:
  0.0 62.8 jit_solution(16703803763204937743)
XLA Ops:
  0.0 0.0 copy-start
  0.0 1.5 %copy.10.refs_4_ = bf16[350,32]{1,0:T(8,128)(2,1)} copy(bf16[350,32]{0,1:T(8,128)(2,1)} %param.11) | data formatting | bytes 44800 | tf_op args[3]
  1.5 0.0 copy-done
  1.5 0.7 %copy.9.refs_2_ = f32[4,3,2048]{2,1,0:T(4,128)} copy(f32[4,3,2048]{2,0,1:T(4,128)S(1)} %copy-done) | data formatting | bytes 196608 | tf_op args[1]
  2.2 59.2 %shard_map.82 = f32[4,2,480]{2,1,0:T(2,128)} custom-call(s32[4,8]{1,0:T(4,128)} %refs_0_.1, f32[1,2048]{1,0:T(1,128)} %bitcast.1, f32[4,3,2048]{2,1,0:T(4,128)} %copy.9.refs_2_, f32[3,350]{1,0:T(4,128)} %refs_3_.1, bf16[350,32]{1,0:T(8,128)(2,1)} %copy.10.refs_4_, s32[4,4,2048]{2,1,0:T(4,128)} %refs_5_.1, f32[4,4,2048]{2,1,0:T(4,128)} %refs_6_.1, ...), custom_call_target="tpu_custom_call" | custom-call | tf_op jit(solution)/shard_map/pallas_call | solution.py:302
  61.5 1.3 %copy.12 = f32[4,2,480]{2,1,0:T(2,128)} copy(f32[4,2,480]{2,1,0:T(2,128)} %shard_map.82) | data formatting | bytes 30720
Async XLA Ops:
  0.0 1.5 %copy-start = (f32[4,3,2048]{2,0,1:T(4,128)S(1)}, f32[4,3,2048]{2,0,1:T(4,128)}, u32[]{:S(2)}) copy-start(f32[4,3,2048]{2,0,1:T(4,128)} %param.9) | copy-start | bytes 294916

commit v3 on v2

--- a/solution.py
+++ b/solution.py
@@ -110,19 +110,20 @@
     slots = (s0, s1)
     iota = lax.broadcasted_iota(jnp.int32, (SLOTS, CHUNK), 0)
 
-    def fringe(t, c):
-        lanes = pl.ds(c * CHUNK, CHUNK)
+    def fringe(t, c, which):
+        lanes = pl.ds(pl.multiple_of(c * CHUNK, CHUNK), CHUNK)
         d0, d1, d2 = pieces(directions_ref[t, :, lanes])
         for j, d in enumerate((d0, d1, d0, d1, d2, d0)):
-            dirs[c % 2, 8 * j : 8 * j + 3] = d
-        u = jnp.dot(pos[:rows], dirs[c % 2].astype(BF), preferred_element_type=F32)
+            dirs[which, 8 * j : 8 * j + 3] = d
+        u = jnp.dot(pos[:rows], dirs[which].astype(BF), preferred_element_type=F32)
         r = u - ((u + MAGIC) - MAGIC)
         z = r * r
         s = (((SIN[3] * z + SIN[2]) * z + SIN[1]) * z + SIN[0]) * r
         n = ((COS[3] * z + COS[2]) * z + COS[1]) * z + COS[0]
-        return s, n
-
-    def fill(t, c, slot, kept):
+        kept_s[t, :, lanes] = s
+        kept_n[t, :, lanes] = n
+
+    def fill(t, c, slot):
         lanes = pl.ds(c * CHUNK, CHUNK)
         spread = jnp.zeros((SLOTS, CHUNK), F32)
         a = amp[:, lanes]
@@ -135,10 +136,7 @@
         amount = jnp.dot(
             jnp.concatenate([b, b], axis=1), jnp.concatenate([hi, lo], axis=0), preferred_element_type=F32
         )
-        if kept:
-            s, n = kept_s[:, lanes], kept_n[:, lanes]
-        else:
-            s, n = fringe(t, c)
+        s, n = kept_s[t, :, lanes], kept_n[t, :, lanes]
         q = amount * s
         slot[:rows] = (amount - q * s).astype(BF)
         slot[wide : wide + rows] = (q * n).astype(BF)
@@ -200,10 +198,15 @@
         sends[e, t] = v.astype(BF)
         far_copy(t, e).start()
 
-    for stage in range(max(bits, chunks)):
-        if stage < chunks:
-            lanes = pl.ds(stage * CHUNK, CHUNK)
-            kept_s[:, lanes], kept_n[:, lanes] = fringe(0, stage)
+    for stage in range(max(bits, TIME_STEPS)):
+        if stage < TIME_STEPS:
+
+            def some(c, carry, t=stage):
+                fringe(t, 2 * c, 0)
+                fringe(t, 2 * c + 1, 1)
+                return carry
+
+            lax.fori_loop(0, chunks // 2, some, 0)
         if stage < bits:
             gather_copy(stage).wait()
             if stage + 1 < bits:
@@ -230,14 +233,14 @@
 
     choose(0)
     for c in range(chunks):
-        fill(0, c, slots[c % 2], True)
+        fill(0, c, slots[c % 2])
         if c > 0:
             add(slots[(c + 1) % 2])
 
     def body(t, carry):
         choose(t)
         for c in range(chunks):
-            fill(t, c, slots[c % 2], False)
+            fill(t, c, slots[c % 2])
             add(slots[(c + 1) % 2])
             if c == 0:
                 finish(t - 1)
@@ -316,8 +319,8 @@
             pltpu.VMEM((2 * wide, CHUNK), BF),
             pltpu.VMEM((2 * wide, CHUNK), BF),
             pltpu.VMEM((2 * wide, 2 * wide), F32),
-            pltpu.VMEM((rows, count), F32),
-            pltpu.VMEM((rows, count), F32),
+            pltpu.VMEM((TIME_STEPS, rows, count), F32),
+            pltpu.VMEM((TIME_STEPS, rows, count), F32),
             pltpu.VMEM((TIME_STEPS, wide, wide), F32),
             pltpu.VMEM((4, 2, wide, pair_count), BF),
             pltpu.VMEM((TIME_STEPS, half, wide), F32),

time: 63 us -> 60.8 us (0.965)
  Pallas kernels: 59.2 us -> 57 us
    pallas_call x1, Pallas kernels: 59.2 us -> 57 us  [local(): pl.pallas_call(lambda *refs: kernel(size, scale, *refs), out_shape=jax.Sh...]
where the time goes in v3:
time: 60.8 us; the launch traced here: 60.5 us
  Pallas kernels  57 us (94%)
  local copies, waits for them, and re-layouts  3.55 us (6%)
    pallas_call x1, Pallas kernels, local(): pl.pallas_call(lambda *refs: kernel(size, scale, *refs), out_shape=jax.Sh...  57 us
    unnamed x5, local copies, waits for them, and re-layouts  3.55 us

profile of v3, /device:TPU:0, one launch (start us, length us, event | category | flops | bytes accessed | tf_op | source)
XLA Modules:
  0.0 60.5 jit_solution(16447480404015889059)
XLA Ops:
  0.0 0.0 copy-start
  0.0 1.5 %copy.10.refs_4_ = bf16[350,32]{1,0:T(8,128)(2,1)} copy(bf16[350,32]{0,1:T(8,128)(2,1)} %param.11) | data formatting | bytes 44800 | tf_op args[3]
  1.5 0.0 copy-done
  1.5 0.7 %copy.9.refs_2_ = f32[4,3,2048]{2,1,0:T(4,128)} copy(f32[4,3,2048]{2,0,1:T(4,128)S(1)} %copy-done) | data formatting | bytes 196608 | tf_op args[1]
  2.2 57.0 %shard_map.82 = f32[4,2,480]{2,1,0:T(2,128)} custom-call(s32[4,8]{1,0:T(4,128)} %refs_0_.1, f32[1,2048]{1,0:T(1,128)} %bitcast.1, f32[4,3,2048]{2,1,0:T(4,128)} %copy.9.refs_2_, f32[3,350]{1,0:T(4,128)} %refs_3_.1, bf16[350,32]{1,0:T(8,128)(2,1)} %copy.10.refs_4_, s32[4,4,2048]{2,1,0:T(4,128)} %refs_5_.1, f32[4,4,2048]{2,1,0:T(4,128)} %refs_6_.1, ...), custom_call_target="tpu_custom_call" | custom-call | tf_op jit(solution)/shard_map/pallas_call | solution.py:305
  59.2 1.3 %copy.12 = f32[4,2,480]{2,1,0:T(2,128)} copy(f32[4,2,480]{2,1,0:T(2,128)} %shard_map.82) | data formatting | bytes 30720
Async XLA Ops:
  0.0 1.5 %copy-start = (f32[4,3,2048]{2,0,1:T(4,128)S(1)}, f32[4,3,2048]{2,0,1:T(4,128)}, u32[]{:S(2)}) copy-start(f32[4,3,2048]{2,0,1:T(4,128)} %param.9) | copy-start | bytes 294916

commit v4 on v3

--- a/solution.py
+++ b/solution.py
@@ -270,17 +270,23 @@
     for e in range(2, far):
         for t in range(TIME_STEPS):
             to_far(t, e)
-    for t in range(TIME_STEPS):
-        far_copy(t, far - 1).wait()
-    total = (acc[...] + gots[far - 1].astype(F32)).astype(BF).reshape(TIME_STEPS * quarter, wide)
     local_iota = lax.broadcasted_iota(jnp.int32, (quarter, pair_count), 0) + mine
-    for m in range(4):
-        for k in range(2):
-            x = jnp.dot(total, ones[m, 1 - k], preferred_element_type=F32)
-            mask = local_iota == quads[m, k : k + 1, :]
-            for t in range(TIME_STEPS):
-                y = jnp.where(mask, x[t * quarter : (t + 1) * quarter], 0.0)
-                res[m, 2 * t + 1 - k : 2 * t + 2 - k, :] = jnp.sum(y, axis=0, keepdims=True)
+
+    def look_up(low, high):
+        for t in range(low, high):
+            far_copy(t, far - 1).wait()
+        total = acc[low:high] + gots[far - 1, low:high].astype(F32)
+        total = total.astype(BF).reshape((high - low) * quarter, wide)
+        for m in range(4):
+            for k in range(2):
+                x = jnp.dot(total, ones[m, 1 - k], preferred_element_type=F32)
+                mask = local_iota == quads[m, k : k + 1, :]
+                for t in range(low, high):
+                    y = jnp.where(mask, x[(t - low) * quarter : (t - low + 1) * quarter], 0.0)
+                    res[m, 2 * t + 1 - k : 2 * t + 2 - k, :] = jnp.sum(y, axis=0, keepdims=True)
+
+    look_up(0, TIME_STEPS - 1)
+    look_up(TIME_STEPS - 1, TIME_STEPS)
     last = []
     for j, other in enumerate(quad):
         last.append(push(res.at[other % 4], got.at[j], rsem.at[0, j], rsem.at[1, j], other))

time: 60.8 us -> 59.6 us (0.980)
  Pallas kernels: 57 us -> 55.8 us
    pallas_call x1, Pallas kernels: 57 us -> 55.8 us  [local(): pl.pallas_call(lambda *refs: kernel(size, scale, *refs), out_shape=jax.Sh...]
where the time goes in v4:
time: 59.6 us; the launch traced here: 59.4 us
  Pallas kernels  55.8 us (94%)
  local copies, waits for them, and re-layouts  3.55 us (6%)
    pallas_call x1, Pallas kernels, local(): pl.pallas_call(lambda *refs: kernel(size, scale, *refs), out_shape=jax.Sh...  55.8 us
    unnamed x5, local copies, waits for them, and re-layouts  3.55 us

profile of v4, /device:TPU:0, one launch (start us, length us, event | category | flops | bytes accessed | tf_op | source)
XLA Modules:
  0.0 59.4 jit_solution(17164153941332075014)
XLA Ops:
  0.0 0.0 copy-start
  0.0 1.5 %copy.10.refs_4_ = bf16[350,32]{1,0:T(8,128)(2,1)} copy(bf16[350,32]{0,1:T(8,128)(2,1)} %param.11) | data formatting | bytes 44800 | tf_op args[3]
  1.5 0.0 copy-done
  1.5 0.7 %copy.9.refs_2_ = f32[4,3,2048]{2,1,0:T(4,128)} copy(f32[4,3,2048]{2,0,1:T(4,128)S(1)} %copy-done) | data formatting | bytes 196608 | tf_op args[1]
  2.2 55.8 %shard_map.82 = f32[4,2,480]{2,1,0:T(2,128)} custom-call(s32[4,8]{1,0:T(4,128)} %refs_0_.1, f32[1,2048]{1,0:T(1,128)} %bitcast.1, f32[4,3,2048]{2,1,0:T(4,128)} %copy.9.refs_2_, f32[3,350]{1,0:T(4,128)} %refs_3_.1, bf16[350,32]{1,0:T(8,128)(2,1)} %copy.10.refs_4_, s32[4,4,2048]{2,1,0:T(4,128)} %refs_5_.1, f32[4,4,2048]{2,1,0:T(4,128)} %refs_6_.1, ...), custom_call_target="tpu_custom_call" | custom-call | tf_op jit(solution)/shard_map/pallas_call | solution.py:311
  58.1 1.3 %copy.12 = f32[4,2,480]{2,1,0:T(2,128)} copy(f32[4,2,480]{2,1,0:T(2,128)} %shard_map.82) | data formatting | bytes 30720
Async XLA Ops:
  0.0 1.5 %copy-start = (f32[4,3,2048]{2,0,1:T(4,128)S(1)}, f32[4,3,2048]{2,0,1:T(4,128)}, u32[]{:S(2)}) copy-start(f32[4,3,2048]{2,0,1:T(4,128)} %param.9) | copy-start | bytes 294916
